TPU v7x, 256 devices: a whole 4x4x8 slice. The times are simulated.
256 devices in a mesh: row: 32 (over y, x, core), col: 8 (over z).
Axes of the slice: x: 4, y: 4, z: 8, core: 2. Of those that a mesh axis runs over, the one named last changes fastest.
Arguments:
- inputs: bfloat16 [4096, 8192], P('row'), may hold values from -1 to 1
- up_codes: int32 [8192, 14336], P('row', 'col'), may hold values from -128 to 127, as said below
- up_scales: float32 [64, 14336], P('row', 'col'), may hold values from 8e-05 to 0.0008
- gate_codes: int32 [8192, 14336], P('row', 'col'), may hold values from -128 to 127, as said below
- gate_scales: float32 [64, 14336], P('row', 'col'), may hold values from 8e-05 to 0.0008
- grad_up: bfloat16 [4096, 14336], P('row', 'col'), may hold values from -1 to 1
- grad_gate: bfloat16 [4096, 14336], P('row', 'col'), may hold values from -1 to 1
Outputs:
- input_grad: bfloat16 [4096, 8192], P('col', 'row')
- up_weight_grad: float32 [8192, 14336], P('row', 'col')
- gate_weight_grad: float32 [8192, 14336], P('row', 'col')
- up_scale_grad: float32 [64, 14336], P('row', 'col')
- gate_scale_grad: float32 [64, 14336], P('row', 'col')
Inputs may be any that keep to these rules, and one draw needn't show every extreme that they name: `up_codes`: integer codes of int8 range held in int32; a share of them sits at each clip end. `gate_codes`: integer codes of int8 range held in int32; a share of them sits at each clip end.
All inputs are finite; a program needn't handle non-finite values.
Results may differ from a plain program's by a relative error of at most 0.017.
Values may be sent and summed in bfloat16 or wider, within the bound.
A program may use at most 128 MiB of HBM per device.

v0:
```python
import jax
import jax.numpy as jnp
from jax import lax
from jax.sharding import PartitionSpec as P

GROUP = 128


def dequant(codes, scales):
    return (codes.astype(jnp.float32) * jnp.repeat(scales, GROUP, axis=0)).astype(jnp.bfloat16)


def scale_grad(hat, codes):
    depth, width = hat.shape
    prod = (hat * codes.astype(jnp.float32)).reshape(depth // GROUP, GROUP, width)
    return jnp.sum(prod, axis=1) / jnp.sqrt(jnp.float32(GROUP * 127))


def outer_rows(slab_rows, piece):
    return lax.dot_general(
        slab_rows, piece, (((0,), (0,)), ((), ())), preferred_element_type=jnp.float32
    )


def back_rows(piece, weight):
    return lax.dot_general(
        piece, weight, (((1,), (1,)), ((), ())), preferred_element_type=jnp.float32
    )


def per_device(inputs, up_codes, up_scales, gate_codes, gate_scales, grad_up, grad_gate):
    w_up = dequant(up_codes, up_scales)
    w_gate = dequant(gate_codes, gate_scales)
    slab = lax.all_to_all(inputs, "row", split_axis=1, concat_axis=0, tiled=True)
    piece = lax.all_gather(grad_up, "row", axis=0, tiled=True)
    slab_rows = slab
    acc_up = outer_rows(slab_rows, piece)
    rows_sum = back_rows(piece, w_up)
    up_hat, rows_sum = (acc_up, rows_sum)
    piece = lax.all_gather(grad_gate, "row", axis=0, tiled=True)
    add_rows_sum = rows_sum
    slab_rows = slab
    acc_gate = outer_rows(slab_rows, piece)
    before = add_rows_sum
    add_rows_sum = before + back_rows(piece, w_gate)
    input_grad = lax.psum_scatter(
        add_rows_sum.astype(jnp.bfloat16), "col", scatter_dimension=0, tiled=True
    )
    up_keep = (up_codes > -128) & (up_codes < 127)
    gate_keep = (gate_codes > -128) & (gate_codes < 127)
    up_weight_grad = jnp.where(up_keep, up_hat, jnp.float32(0.0))
    gate_weight_grad = jnp.where(gate_keep, acc_gate, jnp.float32(0.0))
    return (
        input_grad,
        up_weight_grad,
        gate_weight_grad,
        scale_grad(up_hat, up_codes),
        scale_grad(acc_gate, gate_codes),
    )


def solution(mesh):
    placed = (
        P("row", None),
        P("row", "col"),
        P("row", "col"),
        P("row", "col"),
        P("row", "col"),
        P("row", "col"),
        P("row", "col"),
    )
    return jax.shard_map(
        per_device,
        mesh=mesh,
        in_specs=placed,
        out_specs=(
            P("col", "row"),
            P("row", "col"),
            P("row", "col"),
            P("row", "col"),
            P("row", "col"),
        ),
        check_vma=False,
    )
```

profile of v0, /device:TPU:22, one launch (start us, length us, event | category | flops | bytes accessed | tf_op | source)
XLA Modules:
  0.0 253.1 jit_solution(5900070143420698469)
XLA Ops:
  7.2 0.0 all-gather.3.cloned.1.call-start
  7.2 0.7 all-gather.3.cloned.1.call-update
  7.9 0.0 all-gather.5.cloned.1.call-start
  7.9 0.7 all-gather.5.cloned.1.call-update
  8.6 0.0 reduce-scatter.2.cloned.1.call-start
  8.7 3.2 %copy.14 = bf16[128,8192]{0,1:T(8,128)(2,1)S(1)} copy(bf16[128,8192]{1,0:T(8,128)(2,1)} %param.7) | data formatting | bytes 4194304 | tf_op args[0]
  11.9 39.2 %all_to_all.19 = bf16[128,32,256]{0,2,1:T(8,128)(2,1)} all-to-all(bf16[128,32,256]{0,2,1:T(8,128)(2,1)S(1)} %bitcast.28), channel_id=1, replica_groups=mesh['row'=32,'col'=8] {'row'}, dimensions={1} | all-to-all | bytes 4194304 | tf_op jit(solution)/shard_map/all_to_all | solution.py:34
  51.1 0.0 copy-start.3
  51.1 3.3 %copy.15 = bf16[32,128,256]{2,1,0:T(8,128)(2,1)S(1)} copy(bf16[32,128,256]{1,2,0:T(8,128)(2,1)} %bitcast.27) | data formatting | bytes 4194304 | tf_op jit(solution)/shard_map/all_to_all | solution.py:34
  54.4 44.0 %all-gather.3.cloned.1.call-done = bf16[4096,1792]{1,0:T(8,128)(2,1)} async-done(((bf16[128,1792]{1,0:T(8,128)(2,1)}), bf16[4096,1792]{1,0:T(8,128)(2,1)}) %all-gather.3.cloned.1.call-update) | async-done | bytes 14680080 | tf_op jit(solution)/shard_map/all_gather | solution.py:35
  98.4 0.0 copy-done.3
  98.4 11.4 %and_select_fusion.1 = (f32[256,1792]{1,0:T(8,128)}, bf16[256,1792]{1,0:T(8,128)(2,1)S(1)}, f32[256,1792]{1,0:T(8,128)}) fusion(s32[256,1792]{1,0:T(8,128)} %param.8, f32[2,1792]{1,0:T(2,128)S(1)} %copy-done.3, bf16[4096,256]{1,0:T(8,128)(2,1)S(1)} %bitcast.25, bf16[4096,1792]{1,0:T(8,128)(2,1)} %all-gather.3.cloned.1.call-done), kind=kOutput, calls=%fused_computation.12 | convolution fusion | flops 3761307648 | bytes 23214080 | tf_op jit(solution)/shard_map/dot_general | solution.py:20
  109.7 0.0 copy-start.4
  109.7 16.2 %fusion.4 = f32[256,4096]{1,0:T(8,128)} fusion(bf16[256,1792]{1,0:T(8,128)(2,1)S(1)} %get-tuple-element.23, bf16[4096,1792]{1,0:T(8,128)(2,1)} %all-gather.3.cloned.1.call-done), kind=kOutput, calls=%fused_computation.15 | convolution fusion | flops 3758096384 | bytes 19791872 | tf_op jit(solution)/shard_map/dot_general | solution.py:26
  126.0 47.3 %all-gather.5.cloned.1.call-done = bf16[4096,1792]{1,0:T(8,128)(2,1)} async-done(((bf16[128,1792]{1,0:T(8,128)(2,1)}), bf16[4096,1792]{1,0:T(8,128)(2,1)}) %all-gather.5.cloned.1.call-update) | async-done | bytes 14680080 | tf_op jit(solution)/shard_map/all_gather | solution.py:40
  173.3 0.0 copy-done.4
  173.3 11.4 %and_select_fusion = (f32[256,1792]{1,0:T(8,128)}, bf16[256,1792]{1,0:T(8,128)(2,1)S(1)}, f32[256,1792]{1,0:T(8,128)}) fusion(s32[256,1792]{1,0:T(8,128)} %param.10, f32[2,1792]{1,0:T(2,128)S(1)} %copy-done.4, bf16[4096,256]{1,0:T(8,128)(2,1)S(1)} %bitcast.26, bf16[4096,1792]{1,0:T(8,128)(2,1)} %all-gather.5.cloned.1.call-done), kind=kOutput, calls=%fused_computation.11 | convolution fusion | flops 3761307648 | bytes 23214080 | tf_op jit(solution)/shard_map/dot_general | solution.py:20
  184.7 16.5 %fusion.1 = bf16[4096,256]{0,1:T(8,128)(2,1)} fusion(f32[256,4096]{1,0:T(8,128)} %fusion.4, bf16[256,1792]{1,0:T(8,128)(2,1)S(1)} %get-tuple-element.21, bf16[4096,1792]{1,0:T(8,128)(2,1)} %all-gather.5.cloned.1.call-done), kind=kOutput, calls=%fused_computation.2 | convolution fusion | flops 3760193536 | bytes 21889024 | tf_op jit(solution)/shard_map/dot_general | solution.py:26
  201.2 0.0 copy-start
  201.2 0.0 reduce-scatter.2.cloned.1.call-update
  201.2 1.5 copy-done
  202.7 0.0 copy-start.1
  202.7 0.0 copy-start.2
  202.7 1.9 bitcast_reduce_fusion
  204.6 0.2 copy-done.1
  204.7 0.6 copy-done.2
  205.3 0.2 bitcast_reduce_fusion.1
  205.5 0.6 broadcast_multiply_fusion
  206.1 0.6 broadcast_multiply_fusion.1
  206.7 38.0 %reduce-scatter.2.cloned.1.call-done = bf16[512,256]{0,1:T(8,128)(2,1)} async-done(((bf16[4096,256]{0,1:T(8,128)(2,1)}), bf16[512,256]{0,1:T(8,128)(2,1)}) %reduce-scatter.2.cloned.1.call-update) | async-done | bytes 262160 | tf_op jit(solution)/shard_map/reduce_scatter | solution.py:46
  244.7 1.8 copy.16
Async XLA Ops:
  7.2 91.2 %all-gather.3.cloned.1.call-start = ((), (), s32[]{:S(2)}) async-start(), calls=%async_computation.2 | async-start | bytes 15138816 | tf_op jit(solution)/shard_map/all_gather | solution.py:35
  7.9 165.4 %all-gather.5.cloned.1.call-start = ((), (), s32[]{:S(2)}) async-start(), calls=%async_computation.3 | async-start | bytes 15138816 | tf_op jit(solution)/shard_map/all_gather | solution.py:40
  8.6 236.1 %reduce-scatter.2.cloned.1.call-start = ((), (), s32[]{:S(2)}) async-start(), calls=%async_computation.4 | async-start | bytes 2359296 | tf_op jit(solution)/shard_map/reduce_scatter | solution.py:46
  51.1 47.3 %copy-start.3 = (f32[2,1792]{1,0:T(2,128)S(1)}, f32[2,1792]{1,0:T(2,128)}, u32[]{:S(2)}) copy-start(f32[2,1792]{1,0:T(2,128)} %param.9) | copy-start | bytes 43012
  109.7 63.6 %copy-start.4 = (f32[2,1792]{1,0:T(2,128)S(1)}, f32[2,1792]{1,0:T(2,128)}, u32[]{:S(2)}) copy-start(f32[2,1792]{1,0:T(2,128)} %param.11) | copy-start | bytes 43012
  201.2 1.5 copy-start
  202.7 2.1 copy-start.1
  202.7 2.6 %copy-start.2 = (f32[256,1792]{1,0:T(8,128)S(1)}, f32[256,1792]{1,0:T(8,128)}, u32[]{:S(2)}) copy-start(f32[256,1792]{1,0:T(8,128)} %get-tuple-element.24) | copy-start | bytes 5505028
Sparse Core Ops, SparseCore 0:
  10.5 87.7 all-gather.2
  100.9 72.3 all-gather.4
  201.3 43.3 reduce-scatter.1
where the time goes:
time: 254 us; the launch traced here: 253 us
  waiting for transfers between devices  131 us (52%)
  matrix products  55.5 us (22%)
  blocking collectives  39.2 us (15%)
  between operations  13.8 us (5%)
  local copies, waits for them, and re-layouts  10.5 us (4%)
  other arithmetic  3.33 us (1%)
    all_gather x1, waiting for transfers between devices, per_device(): piece = lax.all_gather(grad_gate, 'row', axis=0, tiled=True)  47.3 us
    all_gather x1, waiting for transfers between devices, per_device(): piece = lax.all_gather(grad_up, 'row', axis=0, tiled=True)  44 us
    all_to_all x1, blocking collectives, per_device(): lax.all_to_all(inputs, 'row', split_axis=1, concat_axis=0, tiled=True)  39.2 us
    reduce_scatter x1, waiting for transfers between devices, per_device(): lax.psum_scatter(add_rows_sum.astype(jnp.bfloat16), 'col', scatter_dimens...  38 us
    dot_general x2, matrix products, back_rows(): lax.dot_general(piece, weight, (((1,), (1,)), ((), ())), preferred_elemen...  32.7 us
    dot_general x2, matrix products, outer_rows(): lax.dot_general(slab_rows, piece, (((0,), (0,)), ((), ())), preferred_ele...  22.8 us
    unnamed x12, local copies, waits for them, and re-layouts  7.21 us
  transfers between devices with their start and end apart: 3, of which 3 were waited for; matrix products, arithmetic and copies ran while one was open for 15% of the time, Pallas kernels for 0%

commit v1 on v0

v1 whole, which is shorter than its diff:
```python
import functools

import jax
import jax.numpy as jnp
from jax import lax
from jax.experimental import pallas as pl
from jax.experimental.pallas import tpu as pltpu
from jax.sharding import PartitionSpec as P

GROUP = 128
NY, NX, NZ = 4, 4, 8
MESH = pl.DeviceIdType.MESH
F32, BF16 = jnp.float32, jnp.bfloat16
HALF = 64

PAIRS = (
    ((-1, 0), (1, 0)),
    ((0, -1), (0, 1)),
    ((0, 0), (2, 0)),
    ((-1, -1), (-1, 1)),
    ((1, -1), (1, 1)),
    ((2, -1), (2, 1)),
    ((0, 2), (-1, 2)),
    ((1, 2), (2, 2)),
)
PLACE = {piece: (p, s) for p, pair in enumerate(PAIRS) for s, piece in enumerate(pair)}
FULL = [(o1, o2) for o2 in (0, -1, 1) for o1 in (-1, 1, 0, 2) if o2 or abs(o1) == 1]
HALVES = [(2, 0), (0, 2), (-1, 2), (1, 2), (2, 2)]
SEM = {(piece, None): i for i, piece in enumerate(FULL)}
for piece in HALVES:
    for part in (0, 1):
        SEM[(piece, part)] = len(SEM)
N_SEM = len(SEM)


def wrap(o):
    return 2 if o in (2, -2) else o


def dot(a, b, ca, cb):
    return lax.dot_general(a, b, (((ca,), (cb,)), ((), ())), preferred_element_type=F32)


def pick(index, table):
    out = jnp.int32(table[0])
    for k in range(1, len(table)):
        out = jnp.where(index == k, jnp.int32(table[k]), out)
    return out


def kernel(
    inputs, up_codes, up_scales, gate_codes, gate_scales, grad_up, grad_gate,
    out_grad, out_up, out_gate, out_up_scale, out_gate_scale,
    g, slab, codes, w, acc, other_hat, own, to_sib, from_sib, to_z, from_z, scales, scale_out,
    g_send, g_recv, own_sem, code_sem, a_send, a_recv, r_send, r_recv,
    s_send, s_recv, w_send, w_recv, x_send, x_recv, z_send, z_recv, h_send, h_recv, o_sem,
):
    row, z = lax.axis_index("row"), lax.axis_index("col")
    c = lax.rem(row, 2)
    chip = row // 2
    y, x = chip // NX, lax.rem(chip, NX)
    sibling = (row + 1 - 2 * c, z)

    def at(dy, dx):
        return (((y + dy + NY) % NY * NX + (x + dx + NX) % NX) * 2 + c, z)

    def along(h, axis, o):
        return at(0, o) if (h == 0) == (axis == 0) else at(o, 0)

    def at_z(k):
        return (row, (z + k + NZ) % NZ)

    def remote(src, dst, send, recv, device):
        return pltpu.make_async_remote_copy(
            src_ref=src, dst_ref=dst, send_sem=send, recv_sem=recv,
            device_id=device, device_id_type=MESH,
        )

    barrier = pltpu.get_barrier_semaphore()
    partners = [at(dy, dx) for dy in range(NY) for dx in range(NX) if dy or dx]
    partners += [sibling] + [at_z(k) for k in range(1, NZ)]
    for device in partners:
        pl.semaphore_signal(barrier, inc=1, device_id=device, device_id_type=MESH)
    code_copies = [
        pltpu.make_async_copy(src, codes.at[i], code_sem.at[i])
        for i, src in enumerate((up_codes, gate_codes))
    ]
    for copy in code_copies:
        copy.start()
    p0, s0 = PLACE[(0, 0)]

    def start_own(keep):
        pltpu.make_async_copy(keep, g.at[p0, c, s0], own_sem.at[0]).start()

    def start_give(give):
        remote(give, g.at[p0, c, s0], own_sem.at[1], own_sem.at[2], sibling).start()

    pl.when(c == 0)(lambda: start_own(grad_up))
    pl.when(c == 1)(lambda: start_own(grad_gate))
    scales[0] = up_scales[...]
    scales[1] = gate_scales[...]
    pl.semaphore_wait(barrier, len(partners))

    pl.when(c == 0)(lambda: start_give(grad_gate))
    pl.when(c == 1)(lambda: start_give(grad_up))

    def a_slot(dy, dx):
        at0, at1 = PLACE[(wrap(dx), wrap(dy))], PLACE[(wrap(dy), wrap(dx))]
        return [jnp.where(c == 0, at0[i], at1[i]) for i in (0, 1)]

    rows_z = pl.ds(pl.multiple_of(z * 16, 16), 16)

    def a_src(dy, dx):
        j = (y + dy + NY) % NY * NX + (x + dx + NX) % NX
        return inputs.at[rows_z, pl.ds(pl.multiple_of(j * 512, 512), 512)]

    offsets = [(dy, dx) for dy in (0, 1, -1, 2) for dx in (0, 1, -1, 2) if dy or dx]
    a_copies = []
    for i, (dy, dx) in enumerate(offsets):
        p, s = a_slot(-dy, -dx)
        copy = remote(
            a_src(dy, dx), slab.at[p, c, s, rows_z], a_send.at[i], a_recv.at[i], at(dy, dx)
        )
        copy.start()
        a_copies.append(copy)
    a_own = pltpu.make_async_copy(a_src(0, 0), slab.at[p0, c, s0, rows_z], a_send.at[15])
    a_own.start()

    def rows_of(part):
        return pl.ds(0, 128) if part is None else pl.ds(part * HALF, HALF)

    def send_piece(h, piece, axis, step, part=None):
        o1, o2 = piece
        there = (wrap(o1 - step), o2) if axis == 0 else (o1, wrap(o2 - step))
        p, s = PLACE[piece]
        q, t = PLACE[there]
        k = SEM[(there, part)]
        rows = rows_of(part)
        remote(
            g.at[p, h, s, rows], g.at[q, h, t, rows], g_send.at[h, k], g_recv.at[h, k],
            along(h, axis, step),
        ).start()

    def piece_copy(h, piece, part=None):
        p, s = PLACE[piece]
        k = SEM[(piece, part)]
        ref = g.at[p, h, s, rows_of(part)]
        return remote(ref, ref, g_send.at[h, k], g_recv.at[h, k], sibling)

    def arrive(h, piece):
        for part in (0, 1) if piece in HALVES else (None,):
            piece_copy(h, piece, part).wait_recv()

    own_piece = g.at[p0, c, s0]
    pltpu.make_async_copy(own_piece, own_piece, own_sem.at[0]).wait()
    sib_piece = g.at[p0, 1 - c, s0]
    remote(sib_piece, sib_piece, own_sem.at[1], own_sem.at[2], sibling).wait_recv()
    for axis in (0, 1):
        for h in (0, 1):
            for step in (1, -1):
                send_piece(h, (0, 0), axis, step)

    for copy in code_copies:
        copy.wait()

    def dequant(matrix, dst):
        def body(i, _):
            r = pl.ds(pl.multiple_of(i * 32, 32), 32)
            scale = scales[matrix, pl.ds(i // 4, 1), :]
            dst[r, :] = (codes[matrix, r, :].astype(F32) * scale).astype(BF16)
            return 0

        lax.fori_loop(0, 8, body, 0)

    dequant(1 - c, w.at[2])
    w_copy = remote(w.at[2], w.at[c], w_send, w_recv, sibling)
    w_copy.start()
    dequant(c, w.at[c])
    acc[...] = jnp.zeros_like(acc)

    def block(k, half=None):
        zb = (z + k + 2 * NZ) % NZ
        r = pl.ds(pl.multiple_of(zb * 16, 16), 16)
        pairs = pl.ds(0, 8) if half is None else pl.ds(half * 4, 4)
        return slab.at[pairs, c, :, r, :], zb

    def ring_copy(k, step, half=None):
        ref, _ = block(k, half)
        i = abs(k) + (0 if step == 1 else 4)
        return remote(ref, ref, r_send.at[i], r_recv.at[i], at_z(step))

    def to_sibling(k, half=None):
        ref, _ = block(k, half)
        i = k + 3 if half is None else 7 + half
        return remote(ref, ref, s_send.at[i], s_recv.at[i], sibling)

    def ring_arrive(k, step, half=None):
        ref, _ = block(k - step, half)
        i = abs(k) + (0 if step == 1 else 4)
        remote(ref, ref, r_send.at[i], r_recv.at[i], at_z(step)).wait_recv()

    a_own.wait()
    for copy in a_copies:
        copy.wait_recv()
    ring_copy(0, 1).start()
    ring_copy(0, -1).start()
    to_sibling(0).start()

    def ring_step(k):
        ring_arrive(-(k - 1), 1)
        ring_copy(-k, 1, 0 if k == 3 else None).start()
        to_sibling(-k).start()
        ring_arrive(k - 1, -1)
        ring_copy(k, -1, 1 if k == 3 else None).start()
        to_sibling(k).start()

    def ring_end():
        ring_arrive(-3, 1, 0)
        to_sibling(-4, 0).start()
        ring_arrive(3, -1, 1)
        to_sibling(4, 1).start()

    def sibling_slab(k, half=None):
        zb = (z + k + 2 * NZ) % NZ
        r = pl.ds(pl.multiple_of(zb * 16, 16), 16)
        pairs = pl.ds(0, 8) if half is None else pl.ds(half * 4, 4)
        ref = slab.at[pairs, 1 - c, :, r, :]
        i = k + 3 if half is None else 7 + half
        return remote(ref, ref, s_send.at[i], s_recv.at[i], sibling)

    ring_step(1)
    remote(w.at[1 - c], w.at[1 - c], w_send, w_recv, sibling).wait_recv()

    def event(pieces):
        for h in (0, 1):
            for piece in pieces:
                arrive(h, piece)
                o1, o2 = piece
                if o2 == 0:
                    if o1 == -1:
                        send_piece(h, piece, 0, 1, 0)
                    if o1 == 1:
                        send_piece(h, piece, 0, -1, 1)
                    send_piece(h, piece, 1, 1)
                    send_piece(h, piece, 1, -1)
                elif o2 == -1:
                    send_piece(h, piece, 1, 1, 0)
                elif o2 == 1:
                    send_piece(h, piece, 1, -1, 1)

    def control(n):
        def when(k, *acts):
            @pl.when(n == k)
            def _():
                for act in acts:
                    act()

        when(0, lambda: event(PAIRS[0]))
        when(2, lambda: ring_step(2), lambda: event(PAIRS[1]))
        when(3, lambda: ring_step(3))

        def slab_all():
            ring_end()
            for k in range(-3, 4):
                sibling_slab(k).wait_recv()
            sibling_slab(-4, 0).wait_recv()
            sibling_slab(4, 1).wait_recv()

        when(4, lambda: event(((2, 0),)), slab_all)
        for p in (3, 4, 5, 6, 7):
            when(2 * p, functools.partial(event, PAIRS[p]))

    def back(n):
        p, h = n // 2, lax.rem(n, 2)
        piece = g[p, h].reshape(256, 1792)
        to_sib[n] = dot(piece, w[1 - c], 1, 1).astype(BF16)
        remote(to_sib.at[n], from_sib.at[n], x_send.at[n], x_recv.at[n], sibling).start()
        own[lax.rem(n, 2)] = dot(piece, w[c], 1, 1)

    def combine(n):
        p, h = n // 2, lax.rem(n, 2)
        remote(to_sib.at[n], from_sib.at[n], x_send.at[n], x_recv.at[n], sibling).wait_recv()
        total = own[lax.rem(n, 2)] + from_sib[n].astype(F32)
        to_z[n] = total.astype(BF16)
        for s in (0, 1):
            o1 = pick(p, [pair[s][0] for pair in PAIRS])
            o2 = pick(p, [pair[s][1] for pair in PAIRS])
            yj = (y + jnp.where(h == 0, o2, o1) + NY) % NY
            xj = (x + jnp.where(h == 0, o1, o2) + NX) % NX
            j = yj * NX + xj
            zd, q = j // 2, lax.rem(j, 2)
            rows = pl.ds(s * 128, 128)

            @pl.when(zd == z)
            def _():
                from_z[z, q, h] = to_z[n, rows, :]

            @pl.when(zd != z)
            def _():
                remote(
                    to_z.at[n, rows], from_z.at[z, q, h], z_send.at[n, s], z_recv.at[z, q, h],
                    (row, zd),
                ).start()

    def hats(n):
        p, h = n // 2, lax.rem(n, 2)
        rows = slab[p, h].reshape(256, 512)
        for t in (0, 896):
            piece = g[p, h, :, :, t : t + 896].reshape(256, 896)
            acc[:, t : t + 896] += dot(rows, piece, 0, 0)

    def hats_end(n):
        return jnp.where(n < 4, 0, jnp.minimum(2 * (n - 3), n + 1))

    def step(n, _):
        control(n)
        back(n)

        @pl.when(n > 0)
        def _():
            combine(n - 1)

        def one(i, _):
            hats(i)
            return 0

        lax.fori_loop(hats_end(n - 1), hats_end(n), one, 0)
        return 0

    lax.fori_loop(0, 16, step, 0)
    combine(15)

    mine = pl.ds(pl.multiple_of(c * 256, 256), 256)
    theirs = pl.ds(pl.multiple_of(256 - c * 256, 256), 256)
    h_copy = remote(acc.at[theirs], other_hat, h_send, h_recv, sibling)
    h_copy.start()

    def finish(matrix, ref):
        for group in (0, 1):
            def body(i, total):
                r = pl.ds(pl.multiple_of(group * GROUP + i * 16, 16), 16)
                hat = ref[r, :]
                code = codes[matrix, r, :]
                ref[r, :] = jnp.where((code > -128) & (code < 127), hat, 0.0)
                prod = hat * code.astype(F32)
                return total + prod[:8] + prod[8:]

            total = lax.fori_loop(0, 8, body, jnp.zeros((8, 1792), F32))
            total = jnp.sum(total, axis=0, keepdims=True)
            scale_out[matrix, group : group + 1, :] = total / jnp.sqrt(F32(GROUP * 127))

    finish(c, acc.at[mine])
    acc_mine = acc.at[mine]

    @pl.when(c == 0)
    def _():
        pltpu.make_async_copy(acc_mine, out_up, o_sem.at[0]).start()

    @pl.when(c == 1)
    def _():
        pltpu.make_async_copy(acc_mine, out_gate, o_sem.at[0]).start()

    h_copy.wait()
    finish(1 - c, other_hat)

    @pl.when(c == 0)
    def _():
        pltpu.make_async_copy(other_hat, out_gate, o_sem.at[1]).start()

    @pl.when(c == 1)
    def _():
        pltpu.make_async_copy(other_hat, out_up, o_sem.at[1]).start()

    out_up_scale[...] = scale_out[0]
    out_gate_scale[...] = scale_out[1]

    remote(own_piece, own_piece, own_sem.at[1], own_sem.at[2], sibling).wait_send()
    for copy in a_copies:
        copy.wait_send()
    w_copy.wait_send()
    for h in (0, 1):
        for (piece, part) in SEM:
            piece_copy(h, piece, part).wait_send()
    for k in (0, 1, 2, 3):
        ring_copy(-k, 1, 0 if k == 3 else None).wait_send()
        ring_copy(k, -1, 1 if k == 3 else None).wait_send()
    for k in range(-3, 4):
        to_sibling(k).wait_send()
    to_sibling(-4, 0).wait_send()
    to_sibling(4, 1).wait_send()

    def sent(n, _):
        remote(to_sib.at[n], from_sib.at[n], x_send.at[n], x_recv.at[n], sibling).wait_send()
        p, h = n // 2, lax.rem(n, 2)
        for s in (0, 1):
            o1 = pick(p, [pair[s][0] for pair in PAIRS])
            o2 = pick(p, [pair[s][1] for pair in PAIRS])
            yj = (y + jnp.where(h == 0, o2, o1) + NY) % NY
            xj = (x + jnp.where(h == 0, o1, o2) + NX) % NX
            j = yj * NX + xj

            @pl.when(j // 2 != z)
            def _():
                ref = to_z.at[n, pl.ds(s * 128, 128)]
                remote(ref, ref, z_send.at[n, s], z_recv.at[0, 0, 0], sibling).wait_send()
        return 0

    lax.fori_loop(0, 16, sent, 0)

    def received(k, _):
        zs = lax.rem(z + k, NZ)
        for q in (0, 1):
            for h in (0, 1):
                ref = from_z.at[zs, q, h]
                remote(ref, ref, z_send.at[0, 0], z_recv.at[zs, q, h], sibling).wait_recv()
        return 0

    lax.fori_loop(1, NZ, received, 0)
    for q in (0, 1):
        for h in (0, 1):
            total = from_z[0, q, h].astype(F32)
            for k in range(1, NZ):
                total = total + from_z[k, q, h].astype(F32)
            r = (2 * q + h) * 128
            out_grad[r : r + 128, :] = total.astype(BF16)

    final = pltpu.make_async_copy(acc_mine, out_up, o_sem.at[0])
    final.wait()
    pltpu.make_async_copy(other_hat, out_gate, o_sem.at[1]).wait()


def per_device(inputs, up_codes, up_scales, gate_codes, gate_scales, grad_up, grad_gate):
    vmem = pl.BlockSpec(memory_space=pltpu.VMEM)
    hbm = pl.BlockSpec(memory_space=pl.ANY)
    dma = pltpu.SemaphoreType.DMA
    return pl.pallas_call(
        kernel,
        out_shape=(
            jax.ShapeDtypeStruct((512, 256), BF16),
            jax.ShapeDtypeStruct((256, 1792), F32),
            jax.ShapeDtypeStruct((256, 1792), F32),
            jax.ShapeDtypeStruct((2, 1792), F32),
            jax.ShapeDtypeStruct((2, 1792), F32),
        ),
        in_specs=[hbm, hbm, vmem, hbm, vmem, hbm, hbm],
        out_specs=(vmem, hbm, hbm, vmem, vmem),
        scratch_shapes=[
            pltpu.VMEM((8, 2, 2, 128, 1792), BF16),
            pltpu.VMEM((8, 2, 2, 128, 512), BF16),
            pltpu.VMEM((2, 256, 1792), jnp.int32),
            pltpu.VMEM((3, 256, 1792), BF16),
            pltpu.VMEM((512, 1792), F32),
            pltpu.VMEM((256, 1792), F32),
            pltpu.VMEM((2, 256, 256), F32),
            pltpu.VMEM((16, 256, 256), BF16),
            pltpu.VMEM((16, 256, 256), BF16),
            pltpu.VMEM((16, 256, 256), BF16),
            pltpu.VMEM((NZ, 2, 2, 128, 256), BF16),
            pltpu.VMEM((2, 2, 1792), F32),
            pltpu.VMEM((2, 2, 1792), F32),
            dma((2, N_SEM)), dma((2, N_SEM)),
            dma((3,)),
            dma((2,)),
            dma((16,)), dma((16,)),
            dma((8,)), dma((8,)),
            dma((9,)), dma((9,)),
            dma, dma,
            dma((16,)), dma((16,)),
            dma((16, 2)), dma((NZ, 2, 2)),
            dma, dma,
            dma((2,)),
        ],
        compiler_params=pltpu.CompilerParams(
            collective_id=0, has_side_effects=True, vmem_limit_bytes=56 * 1024 * 1024
        ),
        name="fused_backward",
    )(inputs, up_codes, up_scales, gate_codes, gate_scales, grad_up, grad_gate)


def solution(mesh):
    placed = (
        P("row", None),
        P("row", "col"),
        P("row", "col"),
        P("row", "col"),
        P("row", "col"),
        P("row", "col"),
        P("row", "col"),
    )
    return jax.shard_map(
        per_device,
        mesh=mesh,
        in_specs=placed,
        out_specs=(
            P("col", "row"),
            P("row", "col"),
            P("row", "col"),
            P("row", "col"),
            P("row", "col"),
        ),
        check_vma=False,
    )
```

time: 254 us -> 131 us (0.52)
  waiting for transfers between devices: 131 us -> 0 us
  Pallas kernels: 0 us -> 122 us
  matrix products: 55.5 us -> 0 us
  blocking collectives: 39.2 us -> 0 us
  between operations: 13.8 us -> 0.65 us
  local copies, waits for them, and re-layouts: 10.5 us -> 7.09 us
  other arithmetic: 3.33 us -> 0 us
    pallas_call x0 -> x1, Pallas kernels: none -> 122 us  [per_device(): pl.pallas_call(kernel, out_shape=(jax.ShapeDtypeStruct((512, 256), BF16),...]
    all_gather x2 -> x0, waiting for transfers between devices: 91.3 us -> none  [the longest x1 47.3 us: per_device(): piece = lax.all_gather(grad_gate, 'row', axis=0, tiled=True)]
    dot_general x4 -> x0, matrix products: 55.5 us -> none  [the longest x2 32.7 us: back_rows(): lax.dot_general(piece, weight, (((1,), (1,)), ((), ())), preferred_elemen...]
    all_to_all x1 -> x0, blocking collectives: 39.2 us -> none  [per_device(): lax.all_to_all(inputs, 'row', split_axis=1, concat_axis=0, tiled=True)]
    reduce_scatter x1 -> x0, waiting for transfers between devices: 38 us -> none  [per_device(): lax.psum_scatter(add_rows_sum.astype(jnp.bfloat16), 'col', scatter_dimens...]
    all_to_all x1 -> x0, local copies, waits for them, and re-layouts: 3.28 us -> none  [per_device(): lax.all_to_all(inputs, 'row', split_axis=1, concat_axis=0, tiled=True)]
    unnamed x12 -> x11, local copies, waits for them, and re-layouts: 7.21 us -> 7.09 us
  transfers between devices with their start and end apart: 3 -> 0, of which waited for: 3 -> 0; matrix products, arithmetic and copies ran while one was open for 15% -> 0% of each run, Pallas kernels for 0% -> 0%
where the time goes in v1:
time: 131 us; the launch traced here: 130 us
  Pallas kernels  122 us (93%)
  local copies, waits for them, and re-layouts  7.09 us (5%)
    pallas_call x1, Pallas kernels, per_device(): pl.pallas_call(kernel, out_shape=(jax.ShapeDtypeStruct((512, 256), BF16),...  122 us
    unnamed x11, local copies, waits for them, and re-layouts  7.09 us

profile of v1, /device:TPU:22, one launch (start us, length us, event | category | flops | bytes accessed | tf_op | source)
XLA Modules:
  0.0 129.9 jit_solution(3539549994160980697)
XLA Ops:
  0.6 122.2 %fused_backward.1 = (bf16[512,256]{1,0:T(8,128)(2,1)}, f32[256,1792]{1,0:T(8,128)}, f32[256,1792]{1,0:T(8,128)}, f32[2,1792]{1,0:T(2,128)}, f32[2,1792]{1,0:T(2,128)}) custom-call(bf16[128,8192]{1,0:T(8,128)(2,1)} %inputs.1, s32[256,1792]{1,0:T(8,128)} %up_codes.1, f32[2,1792]{1,0:T(2,128)} %up_scales.1, s32[256,1792]{1,0:T(8,128)} %gate_codes.1, ...), custom_call_target="tpu_custom_call" | custom-call | tf_op jit(solution)/shard_map/fused_backward/pallas_call | solution.py:436
  122.8 1.7 %copy.17 = bf16[512,256]{1,0:T(8,128)(2,1)} copy(bf16[512,256]{1,0:T(8,128)(2,1)} %get-tuple-element.10) | data formatting | bytes 524288
  124.5 0.0 copy-start
  124.5 3.0 %copy.18 = f32[256,1792]{1,0:T(8,128)} copy(f32[256,1792]{1,0:T(8,128)} %get-tuple-element.11) | data formatting | bytes 3670016
  127.5 0.0 copy-done
  127.5 0.0 copy-start.2
  127.5 0.0 copy-start.1
  127.5 1.2 copy.19
  128.7 0.0 copy-done.2
  128.7 0.6 copy.20
  129.3 0.0 copy-done.1
  129.3 0.6 copy.21
Async XLA Ops:
  124.5 3.0 %copy-start = (f32[256,1792]{1,0:T(8,128)S(1)}, f32[256,1792]{1,0:T(8,128)}, u32[]{:S(2)}) copy-start(f32[256,1792]{1,0:T(8,128)} %get-tuple-element.12) | copy-start | bytes 5505028
  127.5 1.2 copy-start.2
  127.5 1.8 %copy-start.1 = (f32[2,1792]{1,0:T(2,128)S(1)}, f32[2,1792]{1,0:T(2,128)}, u32[]{:S(2)}) copy-start(f32[2,1792]{1,0:T(2,128)} %get-tuple-element.14) | copy-start | bytes 43012

commit v2 on v1

v2 whole, which is shorter than its diff:
```python
import functools

import jax
import jax.numpy as jnp
from jax import lax
from jax.experimental import pallas as pl
from jax.experimental.pallas import tpu as pltpu
from jax.sharding import PartitionSpec as P

GROUP = 128
NY, NX, NZ = 4, 4, 8
MESH = pl.DeviceIdType.MESH
F32, BF16 = jnp.float32, jnp.bfloat16
HALF = 64

ORDER = (
    ((0, 0), (-1, 0), (1, 0), (0, -1), (0, 1), (2, 0), (-1, -1), (-1, 1),
     (1, -1), (1, 1), (0, 2), (2, -1), (2, 1), (-1, 2), (1, 2), (2, 2)),
    ((0, 0), (-1, 0), (1, 0), (0, -1), (0, 1), (2, 0), (-1, -1), (-1, 1),
     (2, -1), (2, 1), (0, 2), (1, -1), (1, 1), (-1, 2), (2, 2), (1, 2)),
)
PLACE = [{piece: n for n, piece in enumerate(order)} for order in ORDER]
FULL = [(o1, o2) for o2 in (0, -1, 1) for o1 in (-1, 1, 0, 2) if o2 or abs(o1) == 1]
HALVES = [(2, 0), (0, 2), (-1, 2), (1, 2), (2, 2)]
SEM = {(piece, None): i for i, piece in enumerate(FULL)}
for piece in HALVES:
    for part in (0, 1):
        SEM[(piece, part)] = len(SEM)
N_SEM = len(SEM)


EARLY, SWITCH = 2, 14


def hop_steps():
    table = [{}, {}, {}, {}, {}]
    for n in range(16):
        step = n + 1
        for k in range(5):
            table[k].setdefault(step, []).append(n)
            step += EARLY if step < SWITCH else 1
    return table


HOPS = hop_steps()
LAST_HOP = max(step for table in HOPS for step in table)


def wrap(o):
    return 2 if o in (2, -2) else o


def dot(a, b, ca, cb):
    return lax.dot_general(a, b, (((ca,), (cb,)), ((), ())), preferred_element_type=F32)


def pick(index, table):
    out = jnp.int32(table[0])
    for k in range(1, len(table)):
        out = jnp.where(index == k, jnp.int32(table[k]), out)
    return out


def kernel(
    inputs, up_codes, up_scales, gate_codes, gate_scales, grad_up, grad_gate,
    out_grad, out_up, out_gate, out_up_scale, out_gate_scale,
    g, slab, codes, w, acc, other_hat, own, to_sib, from_sib, to_z, z_in, scales, scale_out,
    g_send, g_recv, own_sem, code_sem, a_send, a_recv, r_send, r_recv,
    s_send, s_recv, w_send, w_recv, x_send, x_recv, z_send, z_recv, h_send, h_recv, o_sem,
):
    row, z = lax.axis_index("row"), lax.axis_index("col")
    c = lax.rem(row, 2)
    chip = row // 2
    y, x = chip // NX, lax.rem(chip, NX)
    sibling = (row + 1 - 2 * c, z)

    def at(dy, dx):
        return (((y + dy + NY) % NY * NX + (x + dx + NX) % NX) * 2 + c, z)

    def along(h, axis, o):
        return at(0, o) if (h == 0) == (axis == 0) else at(o, 0)

    def at_z(k):
        return (row, (z + k + NZ) % NZ)

    def remote(src, dst, send, recv, device):
        return pltpu.make_async_remote_copy(
            src_ref=src, dst_ref=dst, send_sem=send, recv_sem=recv,
            device_id=device, device_id_type=MESH,
        )

    barrier = pltpu.get_barrier_semaphore()
    partners = [at(dy, dx) for dy in range(NY) for dx in range(NX) if dy or dx]
    partners += [sibling, at_z(1), at_z(-1)]
    for device in partners:
        pl.semaphore_signal(barrier, inc=1, device_id=device, device_id_type=MESH)
    code_copies = [
        pltpu.make_async_copy(src, codes.at[i], code_sem.at[i])
        for i, src in enumerate((up_codes, gate_codes))
    ]
    code_copies += [
        pltpu.make_async_copy(src, scales.at[i], code_sem.at[2 + i])
        for i, src in enumerate((up_scales, gate_scales))
    ]
    for copy in code_copies:
        copy.start()

    def start_own(keep):
        pltpu.make_async_copy(keep, g.at[0, c], own_sem.at[0]).start()

    def start_give(give):
        remote(give, g.at[0, c], own_sem.at[1], own_sem.at[2], sibling).start()

    pl.when(c == 0)(lambda: start_own(grad_up))
    pl.when(c == 1)(lambda: start_own(grad_gate))
    pl.semaphore_wait(barrier, len(partners))

    pl.when(c == 0)(lambda: start_give(grad_gate))
    pl.when(c == 1)(lambda: start_give(grad_up))

    def rows_of(part):
        return pl.ds(0, 128) if part is None else pl.ds(part * HALF, HALF)

    def send_piece(h, piece, axis, step, part=None):
        o1, o2 = piece
        there = (wrap(o1 - step), o2) if axis == 0 else (o1, wrap(o2 - step))
        n, m = PLACE[h][piece], PLACE[h][there]
        k = SEM[(there, part)]
        rows = rows_of(part)
        remote(
            g.at[n, h, rows], g.at[m, h, rows], g_send.at[h, k], g_recv.at[h, k],
            along(h, axis, step),
        ).start()

    def piece_copy(h, piece, part=None):
        k = SEM[(piece, part)]
        ref = g.at[PLACE[h][piece], h, rows_of(part)]
        return remote(ref, ref, g_send.at[h, k], g_recv.at[h, k], sibling)

    def arrive(h, piece):
        for part in (0, 1) if piece in HALVES else (None,):
            piece_copy(h, piece, part).wait_recv()

    own_piece = g.at[0, c]
    pltpu.make_async_copy(own_piece, own_piece, own_sem.at[0]).wait()

    def send_own(h):
        for axis in (0, 1):
            for step in (1, -1):
                send_piece(h, (0, 0), axis, step)

    pl.when(c == 0)(lambda: send_own(0))
    pl.when(c == 1)(lambda: send_own(1))

    def a_slot(dy, dx):
        at0, at1 = PLACE[0][(wrap(dx), wrap(dy))], PLACE[1][(wrap(dy), wrap(dx))]
        return jnp.where(c == 0, at0, at1)

    rows_z = pl.ds(pl.multiple_of(z * 16, 16), 16)

    def a_src(dy, dx):
        j = (y + dy + NY) % NY * NX + (x + dx + NX) % NX
        return inputs.at[rows_z, pl.ds(pl.multiple_of(j * 512, 512), 512)]

    offsets = [(dy, dx) for dy in (0, 1, -1, 2) for dx in (0, 1, -1, 2) if dy or dx]
    a_copies = []
    for i, (dy, dx) in enumerate(offsets):
        n = a_slot(-dy, -dx)
        copy = remote(
            a_src(dy, dx), slab.at[n, c, rows_z], a_send.at[i], a_recv.at[i], at(dy, dx)
        )
        copy.start()
        a_copies.append(copy)
    a_own = pltpu.make_async_copy(a_src(0, 0), slab.at[0, c, rows_z], a_send.at[15])
    a_own.start()

    sib_piece = g.at[0, 1 - c]
    remote(sib_piece, sib_piece, own_sem.at[1], own_sem.at[2], sibling).wait_recv()
    pl.when(c == 0)(lambda: send_own(1))
    pl.when(c == 1)(lambda: send_own(0))

    for copy in code_copies:
        copy.wait()

    def dequant(matrix, dst):
        def body(i, _):
            r = pl.ds(pl.multiple_of(i * 32, 32), 32)
            scale = scales[matrix, pl.ds(i // 4, 1), :]
            dst[r, :] = (codes[matrix, r, :].astype(F32) * scale).astype(BF16)
            return 0

        lax.fori_loop(0, 8, body, 0)

    dequant(1 - c, w.at[2])
    w_copy = remote(w.at[2], w.at[c], w_send, w_recv, sibling)
    w_copy.start()
    dequant(c, w.at[c])
    acc[...] = jnp.zeros_like(acc)

    def block(k, half=None):
        zb = (z + k + 2 * NZ) % NZ
        r = pl.ds(pl.multiple_of(zb * 16, 16), 16)
        pairs = pl.ds(0, 16) if half is None else pl.ds(half * 8, 8)
        return slab.at[pairs, c, r, :], zb

    def ring_copy(k, step, half=None):
        ref, _ = block(k, half)
        i = abs(k) + (0 if step == 1 else 4)
        return remote(ref, ref, r_send.at[i], r_recv.at[i], at_z(step))

    def to_sibling(k, half=None):
        ref, _ = block(k, half)
        i = k + 3 if half is None else 7 + half
        return remote(ref, ref, s_send.at[i], s_recv.at[i], sibling)

    def ring_arrive(k, step, half=None):
        ref, _ = block(k - step, half)
        i = abs(k) + (0 if step == 1 else 4)
        remote(ref, ref, r_send.at[i], r_recv.at[i], at_z(step)).wait_recv()

    a_own.wait()
    for copy in a_copies:
        copy.wait_recv()
    ring_copy(0, 1).start()
    ring_copy(0, -1).start()
    to_sibling(0).start()

    def ring_step(k):
        ring_arrive(-(k - 1), 1)
        ring_copy(-k, 1, 0 if k == 3 else None).start()
        to_sibling(-k).start()
        ring_arrive(k - 1, -1)
        ring_copy(k, -1, 1 if k == 3 else None).start()
        to_sibling(k).start()

    def ring_end():
        ring_arrive(-3, 1, 0)
        to_sibling(-4, 0).start()
        ring_arrive(3, -1, 1)
        to_sibling(4, 1).start()

    def sibling_slab(k, half=None):
        zb = (z + k + 2 * NZ) % NZ
        r = pl.ds(pl.multiple_of(zb * 16, 16), 16)
        pairs = pl.ds(0, 16) if half is None else pl.ds(half * 8, 8)
        ref = slab.at[pairs, 1 - c, r, :]
        i = k + 3 if half is None else 7 + half
        return remote(ref, ref, s_send.at[i], s_recv.at[i], sibling)

    ring_step(1)
    remote(w.at[1 - c], w.at[1 - c], w_send, w_recv, sibling).wait_recv()

    def forward(h, piece):
        o1, o2 = piece
        if o2 == 0 and o1:
            if o1 == -1:
                send_piece(h, piece, 0, 1, 0)
            if o1 == 1:
                send_piece(h, piece, 0, -1, 1)
            if (h, o1) != (1, 1):
                send_piece(h, piece, 1, 1)
                send_piece(h, piece, 1, -1)
            if (h, o1) == (1, 2):
                send_piece(h, (1, 0), 1, 1)
                send_piece(h, (1, 0), 1, -1)
        elif o2 == -1:
            send_piece(h, piece, 1, 1, 0)
        elif o2 == 1:
            send_piece(h, piece, 1, -1, 1)

    def slab_all():
        ring_end()
        for k in range(-3, 4):
            sibling_slab(k).wait_recv()
        sibling_slab(-4, 0).wait_recv()
        sibling_slab(4, 1).wait_recv()

    def control(n):
        def when(k, *acts):
            @pl.when(n == k)
            def _():
                for act in acts:
                    act()

        def item(k):
            for h in (0, 1):
                arrive(h, ORDER[h][k])
                forward(h, ORDER[h][k])

        for k in range(1, 16):
            if k in (1, 3, 6, 8, 11):
                when(k, functools.partial(item, k), functools.partial(item, k + 1))
            elif k not in (2, 4, 7, 9, 12):
                when(k, functools.partial(item, k))
        when(3, lambda: ring_step(2))
        when(4, lambda: ring_step(3))
        when(5, slab_all)

    def back(n):
        piece = g[n].reshape(256, 1792)
        to_sib[n] = dot(piece, w[1 - c], 1, 1).astype(BF16)
        remote(to_sib.at[n], from_sib.at[n], x_send.at[n], x_recv.at[n], sibling).start()
        own[lax.rem(n, 2)] = dot(piece, w[c], 1, 1)

    def owner(n, h):
        o1 = pick(n, [piece[0] for piece in ORDER[h]])
        o2 = pick(n, [piece[1] for piece in ORDER[h]])
        yj, xj = (y + (o1, o2)[1 - h] + NY) % NY, (x + (o1, o2)[h] + NX) % NX
        j = yj * NX + xj
        return (j // 2 - z + NZ) % NZ, lax.rem(j, 2)

    def combine(n):
        remote(to_sib.at[n], from_sib.at[n], x_send.at[n], x_recv.at[n], sibling).wait_recv()
        total = own[lax.rem(n, 2)] + from_sib[n].astype(F32)
        to_z[n] = total.astype(BF16)

    def z_copy(n, h, d, rows):
        return remote(
            to_z.at[n, pl.ds(h * 128 + rows[0], rows[1])], z_in.at[n, h, d, pl.ds(*rows)],
            z_send.at[n, h, d], z_recv.at[n, h, d], at_z(1 - 2 * d),
        )

    def out_rows(q, h):
        return pl.ds(pl.multiple_of((2 * q + h) * 128, 128), 128)

    def hop(n, h, distance):
        delta, q = owner(n, h)
        if distance == 4:
            @pl.when(delta == 4)
            def _():
                z_copy(n, h, 0, (0, HALF)).start()
                z_copy(n, h, 1, (HALF, HALF)).start()
        elif distance:
            d = jnp.where(delta < 4, 0, 1)

            @pl.when((delta == distance) | (delta == NZ - distance))
            def _():
                rows = (d * HALF, HALF) if distance == 3 else (0, 128)
                z_copy(n, h, d, rows).wait_recv()
                here = pl.ds(h * 128 + rows[0], rows[1])
                total = to_z[n, here, :].astype(F32) + z_in[n, h, d, pl.ds(*rows), :].astype(F32)
                to_z[n, here, :] = total.astype(BF16)
                z_copy(n, h, d, (0, 128)).start()
        else:
            @pl.when(delta == 0)
            def _():
                total = to_z[n, pl.ds(h * 128, 128), :].astype(F32)
                for d in (0, 1):
                    z_copy(n, h, d, (0, 128)).wait_recv()
                    total = total + z_in[n, h, d].astype(F32)
                out_grad[out_rows(q, h), :] = total.astype(BF16)

    def hops(n):
        for k in range(5):
            for slot in range(max(len(items) for items in HOPS[k].values())):
                items = [(HOPS[k].get(t, []) + [-1, -1, -1])[slot] for t in range(16)]
                if max(items) < 0:
                    continue
                m = pick(n, items)

                @pl.when(m >= 0)
                def _():
                    for h in (0, 1):
                        hop(m, h, 4 - k)

    def late_hops(step):
        for k in range(5):
            for m in HOPS[k].get(step, []):
                for h in (0, 1):
                    hop(jnp.int32(m), h, 4 - k)

    def hats(n):
        rows = slab[n].reshape(256, 512)
        for t in (0, 896):
            piece = g[n, :, :, t : t + 896].reshape(256, 896)
            acc[:, t : t + 896] += dot(rows, piece, 0, 0)

    def early_sends():
        remote(own_piece, own_piece, own_sem.at[1], own_sem.at[2], sibling).wait_send()
        for copy in a_copies:
            copy.wait_send()
        w_copy.wait_send()
        for k in (0, 1, 2, 3):
            ring_copy(-k, 1, 0 if k == 3 else None).wait_send()
            ring_copy(k, -1, 1 if k == 3 else None).wait_send()
        for k in range(-3, 4):
            to_sibling(k).wait_send()
        to_sibling(-4, 0).wait_send()
        to_sibling(4, 1).wait_send()

    def hats_end(n):
        return jnp.where(n < 5, 0, jnp.minimum(2 * (n - 4), n + 1))

    def step(n, _):

        control(n)
        back(n)
        pl.when(n > 0)(lambda: combine(n - 1))
        hops(n)

        def one(i, _):
            hats(i)
            return 0

        lax.fori_loop(hats_end(n - 1), hats_end(n), one, 0)
        pl.when(n == 12)(early_sends)
        return 0

    lax.fori_loop(0, 16, step, 0)
    combine(15)
    late_hops(16)

    mine = pl.ds(pl.multiple_of(c * 256, 256), 256)
    theirs = pl.ds(pl.multiple_of(256 - c * 256, 256), 256)
    h_copy = remote(acc.at[theirs], other_hat, h_send, h_recv, sibling)
    h_copy.start()

    def finish(matrix, ref):
        for group in (0, 1):
            def body(i, total):
                r = pl.ds(pl.multiple_of(group * GROUP + i * 16, 16), 16)
                hat = ref[r, :]
                code = codes[matrix, r, :]
                ref[r, :] = jnp.where((code > -128) & (code < 127), hat, 0.0)
                prod = hat * code.astype(F32)
                return total + prod[:8] + prod[8:]

            total = lax.fori_loop(0, 8, body, jnp.zeros((8, 1792), F32))
            total = jnp.sum(total, axis=0, keepdims=True)
            scale_out[matrix, group : group + 1, :] = total / jnp.sqrt(F32(GROUP * 127))

    finish(c, acc.at[mine])
    acc_mine = acc.at[mine]

    @pl.when(c == 0)
    def _():
        pltpu.make_async_copy(acc_mine, out_up, o_sem.at[0]).start()

    @pl.when(c == 1)
    def _():
        pltpu.make_async_copy(acc_mine, out_gate, o_sem.at[0]).start()

    late_hops(17)
    h_copy.wait()
    finish(1 - c, other_hat)
    late_hops(18)

    @pl.when(c == 0)
    def _():
        pltpu.make_async_copy(other_hat, out_gate, o_sem.at[1]).start()

    @pl.when(c == 1)
    def _():
        pltpu.make_async_copy(other_hat, out_up, o_sem.at[1]).start()

    out_up_scale[...] = scale_out[0]
    out_gate_scale[...] = scale_out[1]

    def sent(n, _):
        remote(to_sib.at[n], from_sib.at[n], x_send.at[n], x_recv.at[n], sibling).wait_send()
        for h in (0, 1):
            delta, _ = owner(n, h)

            @pl.when(delta == 4)
            def _():
                z_copy(n, h, 0, (0, HALF)).wait_send()
                z_copy(n, h, 1, (HALF, HALF)).wait_send()

            @pl.when((delta != 0) & (delta != 4))
            def _():
                z_copy(n, h, jnp.where(delta < 4, 0, 1), (0, 128)).wait_send()
        return 0

    for h in (0, 1):
        for piece, part in SEM:
            piece_copy(h, piece, part).wait_send()
    late_hops(19)
    lax.fori_loop(0, 14, sent, 0)
    for last in range(20, LAST_HOP + 1):
        late_hops(last)
    lax.fori_loop(14, 16, sent, 0)
    final = pltpu.make_async_copy(acc_mine, out_up, o_sem.at[0])
    final.wait()
    pltpu.make_async_copy(other_hat, out_gate, o_sem.at[1]).wait()


def emit(*refs):
    sources, results, sems = refs[:5], refs[5:10], refs[10]
    copies = [
        pltpu.make_async_copy(a, b, sems.at[i]) for i, (a, b) in enumerate(zip(sources, results))
    ]
    for copy in copies:
        copy.start()
    for copy in copies:
        copy.wait()


def per_device(inputs, up_codes, up_scales, gate_codes, gate_scales, grad_up, grad_gate):
    vmem = pl.BlockSpec(memory_space=pltpu.VMEM)
    hbm = pl.BlockSpec(memory_space=pltpu.HBM)
    anywhere = pl.BlockSpec(memory_space=pl.ANY)
    dma = pltpu.SemaphoreType.DMA
    pinned = [
        pltpu.with_memory_space_constraint(a, pltpu.HBM)
        for a in (inputs, up_codes, up_scales, gate_codes, gate_scales, grad_up, grad_gate)
    ]
    results = pl.pallas_call(
        kernel,
        out_shape=(
            jax.ShapeDtypeStruct((512, 256), BF16),
            jax.ShapeDtypeStruct((256, 1792), F32),
            jax.ShapeDtypeStruct((256, 1792), F32),
            jax.ShapeDtypeStruct((2, 1792), F32),
            jax.ShapeDtypeStruct((2, 1792), F32),
        ),
        in_specs=[hbm] * 7,
        out_specs=(vmem, anywhere, anywhere, vmem, vmem),
        scratch_shapes=[
            pltpu.VMEM((16, 2, 128, 1792), BF16),
            pltpu.VMEM((16, 2, 128, 512), BF16),
            pltpu.VMEM((2, 256, 1792), jnp.int32),
            pltpu.VMEM((3, 256, 1792), BF16),
            pltpu.VMEM((512, 1792), F32),
            pltpu.VMEM((256, 1792), F32),
            pltpu.VMEM((2, 256, 256), F32),
            pltpu.VMEM((16, 256, 256), BF16),
            pltpu.VMEM((16, 256, 256), BF16),
            pltpu.VMEM((16, 256, 256), BF16),
            pltpu.VMEM((16, 2, 2, 128, 256), BF16),
            pltpu.VMEM((2, 2, 1792), F32),
            pltpu.VMEM((2, 2, 1792), F32),
            dma((2, N_SEM)), dma((2, N_SEM)),
            dma((3,)),
            dma((4,)),
            dma((16,)), dma((16,)),
            dma((8,)), dma((8,)),
            dma((9,)), dma((9,)),
            dma, dma,
            dma((16,)), dma((16,)),
            dma((16, 2, 2)), dma((16, 2, 2)),
            dma, dma,
            dma((2,)),
        ],
        compiler_params=pltpu.CompilerParams(
            collective_id=0, has_side_effects=True, vmem_limit_bytes=48 * 1024 * 1024
        ),
        name="fused_backward",
    )(*pinned)
    return tuple(
        pl.pallas_call(
            emit,
            out_shape=tuple(jax.ShapeDtypeStruct(r.shape, r.dtype) for r in results),
            in_specs=[anywhere] * 5,
            out_specs=(hbm,) * 5,
            scratch_shapes=[dma((5,))],
            compiler_params=pltpu.CompilerParams(vmem_limit_bytes=1024 * 1024),
            name="emit",
        )(*results)
    )


def solution(mesh):
    placed = (
        P("row", None),
        P("row", "col"),
        P("row", "col"),
        P("row", "col"),
        P("row", "col"),
        P("row", "col"),
        P("row", "col"),
    )
    return jax.shard_map(
        per_device,
        mesh=mesh,
        in_specs=placed,
        out_specs=(
            P("col", "row"),
            P("row", "col"),
            P("row", "col"),
            P("row", "col"),
            P("row", "col"),
        ),
        check_vma=False,
    )
```

time: 131 us -> 122 us (0.931); the launches traced: 130 us -> 122 us
  local copies, waits for them, and re-layouts: 7.09 us -> 0 us
    unnamed x11 -> x0, local copies, waits for them, and re-layouts: 7.09 us -> none
    pallas_call x1, Pallas kernels: 122 us -> 120 us  [per_device(): pl.pallas_call(kernel, out_shape=(jax.ShapeDtypeStruct((512, 256), BF16),...]
    pallas_call x0 -> x1, Pallas kernels: none -> 1.97 us  [per_device(): pl.pallas_call(emit, out_shape=tuple((jax.ShapeDtypeStruct(r.shape, r.dty...]
where the time goes in v2:
time: 122 us
  Pallas kernels  122 us (100%)
    pallas_call x1, Pallas kernels, per_device(): pl.pallas_call(kernel, out_shape=(jax.ShapeDtypeStruct((512, 256), BF16),...  120 us

profile of v2, /device:TPU:22, one launch (start us, length us, event | category | flops | bytes accessed | tf_op | source)
XLA Modules:
  0.0 122.3 jit_solution(17823468977032111380)
XLA Ops:
  0.6 119.7 %fused_backward.1 = (bf16[512,256]{1,0:T(8,128)(2,1)S(1)}, f32[256,1792]{1,0:T(8,128)S(1)}, f32[256,1792]{1,0:T(8,128)S(1)}, f32[2,1792]{1,0:T(2,128)S(1)}, f32[2,1792]{1,0:T(2,128)S(1)}) custom-call(bf16[128,8192]{1,0:T(8,128)(2,1)} %inputs.1, s32[256,1792]{1,0:T(8,128)} %up_codes.1, f32[2,1792]{1,0:T(2,128)} %up_scales.1, s32[256,1792]{1,0:T(8,128)} %gate_codes.1, ...), custom_call_target="tpu_custom_call" | custom-call | tf_op jit(solution)/shard_map/fused_backward/pallas_call | solution.py:507
  120.3 2.0 %emit.1 = (bf16[512,256]{1,0:T(8,128)(2,1)}, f32[256,1792]{1,0:T(8,128)}, f32[256,1792]{1,0:T(8,128)}, f32[2,1792]{1,0:T(2,128)}, f32[2,1792]{1,0:T(2,128)}) custom-call(bf16[512,256]{1,0:T(8,128)(2,1)S(1)} %get-tuple-element.10.refs_0_, f32[256,1792]{1,0:T(8,128)S(1)} %get-tuple-element.11.refs_1_, f32[256,1792]{1,0:T(8,128)S(1)} %get-tuple-element.12.refs_2_, ...), custom_call_target="tpu_custom_call" | custom-call | tf_op jit(solution)/shard_map/emit/pallas_call | solution.py:550

commit v3 on v2

--- a/solution.py
+++ b/solution.py
@@ -20,6 +20,9 @@
      (2, -1), (2, 1), (0, 2), (1, -1), (1, 1), (-1, 2), (2, 2), (1, 2)),
 )
 PLACE = [{piece: n for n, piece in enumerate(order)} for order in ORDER]
+PACKED = [
+    sum((o % 4) * 4 ** i for i, o in enumerate(ORDER[0][n] + ORDER[1][n])) for n in range(16)
+]
 FULL = [(o1, o2) for o2 in (0, -1, 1) for o1 in (-1, 1, 0, 2) if o2 or abs(o1) == 1]
 HALVES = [(2, 0), (0, 2), (-1, 2), (1, 2), (2, 2)]
 SEM = {(piece, None): i for i, piece in enumerate(FULL)}
@@ -74,11 +77,15 @@
     y, x = chip // NX, lax.rem(chip, NX)
     sibling = (row + 1 - 2 * c, z)
 
+    rem = lambda a, b: lax.rem(a, jnp.int32(b))
+
     def at(dy, dx):
-        return (((y + dy + NY) % NY * NX + (x + dx + NX) % NX) * 2 + c, z)
+        return ((rem(y + dy + NY, NY) * NX + rem(x + dx + NX, NX)) * 2 + c, z)
+
+    beside = {(dy, dx): at(dy, dx) for dy, dx in ((0, 1), (0, -1), (1, 0), (-1, 0))}
 
     def along(h, axis, o):
-        return at(0, o) if (h == 0) == (axis == 0) else at(o, 0)
+        return beside[(0, o) if (h == 0) == (axis == 0) else (o, 0)]
 
     def at_z(k):
         return (row, (z + k + NZ) % NZ)
@@ -303,11 +310,17 @@
         own[lax.rem(n, 2)] = dot(piece, w[c], 1, 1)
 
     def owner(n, h):
-        o1 = pick(n, [piece[0] for piece in ORDER[h]])
-        o2 = pick(n, [piece[1] for piece in ORDER[h]])
-        yj, xj = (y + (o1, o2)[1 - h] + NY) % NY, (x + (o1, o2)[h] + NX) % NX
-        j = yj * NX + xj
-        return (j // 2 - z + NZ) % NZ, lax.rem(j, 2)
+        if isinstance(n, int):
+            o1, o2 = ORDER[h][n]
+        else:
+            packed = pick(n, PACKED)
+            o1, o2 = rem(packed // (1, 16)[h], 4), rem(packed // (4, 64)[h], 4)
+        j = rem(y + (o1, o2)[1 - h] + NY, NY) * NX + rem(x + (o1, o2)[h] + NX, NX)
+        return rem(j // 2 - z + NZ, NZ), rem(j, 2)
+
+    def owners(n):
+        far, chips = zip(*(owner(n, h) for h in (0, 1)))
+        return far[0] + 8 * chips[0] + 16 * far[1] + 128 * chips[1]
 
     def combine(n):
         remote(to_sib.at[n], from_sib.at[n], x_send.at[n], x_recv.at[n], sibling).wait_recv()
@@ -323,8 +336,11 @@
     def out_rows(q, h):
         return pl.ds(pl.multiple_of((2 * q + h) * 128, 128), 128)
 
-    def hop(n, h, distance):
-        delta, q = owner(n, h)
+    def hop(n, h, distance, code=None):
+        if code is None:
+            delta, q = owner(n, h)
+        else:
+            delta, q = rem(code // (1, 16)[h], NZ), rem(code // (8, 128)[h], 2)
         if distance == 4:
             @pl.when(delta == 4)
             def _():
@@ -350,24 +366,24 @@
                     total = total + z_in[n, h, d].astype(F32)
                 out_grad[out_rows(q, h), :] = total.astype(BF16)
 
-    def hops(n):
+    def hops(n, codes):
         for k in range(5):
-            for slot in range(max(len(items) for items in HOPS[k].values())):
-                items = [(HOPS[k].get(t, []) + [-1, -1, -1])[slot] for t in range(16)]
-                if max(items) < 0:
-                    continue
-                m = pick(n, items)
-
-                @pl.when(m >= 0)
-                def _():
+            m = n - 1 - EARLY * k
+
+            @pl.when(m >= 0)
+            def _():
+                for h in (0, 1):
+                    hop(m, h, 4 - k, codes[EARLY * k])
+
+        for step in range(SWITCH, 16):
+            pl.when(n == step)(functools.partial(late_hops, step, EARLY))
+
+    def late_hops(step, regular=None):
+        for k in range(5):
+            for m in HOPS[k].get(step, []):
+                if regular is None or m != step - 1 - regular * k:
                     for h in (0, 1):
                         hop(m, h, 4 - k)
-
-    def late_hops(step):
-        for k in range(5):
-            for m in HOPS[k].get(step, []):
-                for h in (0, 1):
-                    hop(jnp.int32(m), h, 4 - k)
 
     def hats(n):
         rows = slab[n].reshape(256, 512)
@@ -391,12 +407,13 @@
     def hats_end(n):
         return jnp.where(n < 5, 0, jnp.minimum(2 * (n - 4), n + 1))
 
-    def step(n, _):
+    def step(n, codes):
+        codes = (owners(n - 1),) + codes[:-1]
 
         control(n)
         back(n)
         pl.when(n > 0)(lambda: combine(n - 1))
-        hops(n)
+        hops(n, codes)
 
         def one(i, _):
             hats(i)
@@ -404,9 +421,9 @@
 
         lax.fori_loop(hats_end(n - 1), hats_end(n), one, 0)
         pl.when(n == 12)(early_sends)
-        return 0
-
-    lax.fori_loop(0, 16, step, 0)
+        return codes
+
+    lax.fori_loop(0, 16, step, (jnp.int32(0),) * (4 * EARLY + 1))
     combine(15)
     late_hops(16)
 
@@ -456,7 +473,7 @@
     out_up_scale[...] = scale_out[0]
     out_gate_scale[...] = scale_out[1]
 
-    def sent(n, _):
+    def sent(n):
         remote(to_sib.at[n], from_sib.at[n], x_send.at[n], x_recv.at[n], sibling).wait_send()
         for h in (0, 1):
             delta, _ = owner(n, h)
@@ -469,16 +486,17 @@
             @pl.when((delta != 0) & (delta != 4))
             def _():
                 z_copy(n, h, jnp.where(delta < 4, 0, 1), (0, 128)).wait_send()
-        return 0
 
     for h in (0, 1):
         for piece, part in SEM:
             piece_copy(h, piece, part).wait_send()
     late_hops(19)
-    lax.fori_loop(0, 14, sent, 0)
+    for n in range(14):
+        sent(n)
     for last in range(20, LAST_HOP + 1):
         late_hops(last)
-    lax.fori_loop(14, 16, sent, 0)
+    for n in (14, 15):
+        sent(n)
     final = pltpu.make_async_copy(acc_mine, out_up, o_sem.at[0])
     final.wait()
     pltpu.make_async_copy(other_hat, out_gate, o_sem.at[1]).wait()

time: 122 us -> 120 us (0.984)
  Pallas kernels: 122 us -> 120 us
    pallas_call x1, Pallas kernels: 120 us -> 118 us  [per_device(): pl.pallas_call(kernel, out_shape=(jax.ShapeDtypeStruct((512, 256), BF16),...]
where the time goes in v3:
time: 120 us
  Pallas kernels  120 us (100%)
    pallas_call x1, Pallas kernels, per_device(): pl.pallas_call(kernel, out_shape=(jax.ShapeDtypeStruct((512, 256), BF16),...  118 us

profile of v3, /device:TPU:22, one launch (start us, length us, event | category | flops | bytes accessed | tf_op | source)
XLA Modules:
  0.0 120.4 jit_solution(4466669636002462746)
XLA Ops:
  0.6 117.8 %fused_backward.1 = (bf16[512,256]{1,0:T(8,128)(2,1)S(1)}, f32[256,1792]{1,0:T(8,128)S(1)}, f32[256,1792]{1,0:T(8,128)S(1)}, f32[2,1792]{1,0:T(2,128)S(1)}, f32[2,1792]{1,0:T(2,128)S(1)}) custom-call(bf16[128,8192]{1,0:T(8,128)(2,1)} %inputs.1, s32[256,1792]{1,0:T(8,128)} %up_codes.1, f32[2,1792]{1,0:T(2,128)} %up_scales.1, s32[256,1792]{1,0:T(8,128)} %gate_codes.1, ...), custom_call_target="tpu_custom_call" | custom-call | tf_op jit(solution)/shard_map/fused_backward/pallas_call | solution.py:525
  118.4 2.0 %emit.1 = (bf16[512,256]{1,0:T(8,128)(2,1)}, f32[256,1792]{1,0:T(8,128)}, f32[256,1792]{1,0:T(8,128)}, f32[2,1792]{1,0:T(2,128)}, f32[2,1792]{1,0:T(2,128)}) custom-call(bf16[512,256]{1,0:T(8,128)(2,1)S(1)} %get-tuple-element.10.refs_0_, f32[256,1792]{1,0:T(8,128)S(1)} %get-tuple-element.11.refs_1_, f32[256,1792]{1,0:T(8,128)S(1)} %get-tuple-element.12.refs_2_, ...), custom_call_target="tpu_custom_call" | custom-call | tf_op jit(solution)/shard_map/emit/pallas_call | solution.py:568
